TPU v7x, 32 devices: a whole 2x2x4 slice. The times are simulated.
32 devices in a mesh: row: 8 (over z, core), col: 4 (over y, x).
Axes of the slice: x: 2, y: 2, z: 4, core: 2. Of those that a mesh axis runs over, the one named last changes fastest.
Arguments:
- tensor: float32 [12, 4096, 2048], P(None, 'row', 'col'), may hold values from -6 to 6
- factor_b: float32 [2048, 128], P(('col', 'row')), may hold values from -0.125 to 0.125
- factor_c: float32 [12, 128], replicated, may hold values from -1.75 to 1.75
Outputs:
- a_update: float32 [4096, 128], P(('row', 'col'))
- b_update: float32 [2048, 128], P(('col', 'row'))
All inputs are finite; a program needn't handle non-finite values.
Results may differ from a plain program's by a relative error of at most 0.00012.
Values sent between devices are 32-bit elements; how exact they have to be, the bound alone decides.
A program may use at most 64 MiB of HBM per device.

v0:
```python
import jax
import jax.numpy as jnp
from jax import lax
from jax.sharding import PartitionSpec as P

EPSILON = 1e-06


def solve_system(rhs, system):
    highest = lax.Precision.HIGHEST
    lower = jnp.linalg.cholesky(system)
    inverse = jax.scipy.linalg.cho_solve(
        (lower, True), jnp.eye(system.shape[0], dtype=system.dtype)
    )
    return jnp.dot(rhs, inverse, precision=highest)


def gram_of(matrix):
    return jnp.dot(matrix.T, matrix, precision=lax.Precision.HIGHEST)


def per_device(tensor, factor_b, factor_c):
    highest = lax.Precision.HIGHEST
    rows_block = tensor.shape[1]
    cols_block = tensor.shape[2]
    rank_width = factor_c.shape[1]
    owned_a = rows_block // lax.axis_size("col")
    owned_b = cols_block // lax.axis_size("row")
    c_gram = gram_of(factor_c)
    empty_b = jnp.zeros((cols_block, rank_width), jnp.float32)
    empty_gram = jnp.zeros((rank_width, rank_width), jnp.float32)
    piece = lax.all_gather(factor_b, "row", axis=0, tiled=True)
    block = tensor
    khatri = factor_c[:, None, :] * piece[None, :, :]
    partial_a = jnp.einsum("kij,kjr->ir", block, khatri, precision=highest)
    gram_part = gram_of(piece)
    gram_b = lax.psum(gram_part, "col")
    whole_a = lax.psum(partial_a, "col")
    summed_a = lax.dynamic_slice_in_dim(whole_a, lax.axis_index("col") * owned_a, owned_a, 0)
    a_update = solve_system(summed_a, c_gram * gram_b)
    squares = lax.psum(jnp.sum(a_update * a_update, axis=0), ("row", "col"))
    factor_a = a_update / jnp.sqrt(squares + EPSILON)
    piece = lax.all_gather(factor_a, "col", axis=0, tiled=True)
    block = tensor
    khatri = factor_c[:, None, :] * piece[None, :, :]
    partial_b = empty_b + jnp.einsum("kij,kir->jr", block, khatri, precision=highest)
    gram_piece = empty_gram + gram_of(piece)
    gram_a = lax.psum(gram_piece, "row")
    whole_b = lax.psum(partial_b, "row")
    summed_b = lax.dynamic_slice_in_dim(whole_b, lax.axis_index("row") * owned_b, owned_b, 0)
    b_update = solve_system(summed_b, c_gram * gram_a)
    return (a_update, b_update)


def solution(mesh):
    placed = (P(None, "row", "col"), P(("col", "row"), None), P())
    return jax.shard_map(
        per_device,
        mesh=mesh,
        in_specs=placed,
        out_specs=(P(("row", "col"), None), P(("col", "row"), None)),
        check_vma=False,
    )
```

profile of v0, /device:TPU:0, one launch (start us, length us, event | category | flops | bytes accessed | tf_op | source)
XLA Modules:
  0.0 263.5 jit_solution(6227931069978276049)
XLA Ops:
  7.2 16.1 %all_gather.6 = f32[512,128]{1,0:T(8,128)S(1)} all-gather(f32[64,128]{1,0:T(8,128)} %param.7), channel_id=1, replica_groups=mesh['row'=8,'col'=4] {'row'}, dimensions={0}, use_global_device_ids=true | all-gather | bytes 294912 | tf_op jit(solution)/shard_map/all_gather | solution.py:32
  23.3 1.2 fusion.35
  24.5 18.3 %fusion.8 = f32[512,128]{0,1:T(8,128)} fusion(f32[12,512,512]{2,1,0:T(8,128)} %param.6, f32[512,128]{1,0:T(8,128)S(1)} %all_gather.6, f32[12,128]{1,0:T(8,128)} %param.8), kind=kOutput, calls=%fused_computation.8 | convolution fusion | flops 4832624640 | bytes 13113344 | tf_op jit(solution)/shard_map/kij,kjr->ir/dot_general | solution.py:35
  42.9 0.2 all-reduce.5.cloned.1.call-start
  43.1 44.7 %all-reduce.7.cloned.1.call-done = (f32[128,128]{0,1:T(8,128)}, f32[512,128]{0,1:T(8,128)}) async-done(((f32[128,128]{0,1:T(8,128)}, f32[512,128]{0,1:T(8,128)}), (f32[128,128]{0,1:T(8,128)}, f32[512,128]{0,1:T(8,128)})) %all-reduce.7.cloned.1.call-update) | async-done | bytes 327696 | tf_op jit(solution)/shard_map/psum | solution.py:37
  87.8 1.1 fusion.34
  89.1 11.7 %cholesky.44 = f32[128,128]{1,0:T(8,128)S(1)} custom-call(f32[128,128]{1,0:T(8,128)S(1)} %fusion.27), custom_call_target="Cholesky" | custom-call | tf_op jit(solution)/shard_map/jit(cholesky)/cholesky | solution.py:11
  100.8 0.6 compare_reduce_fusion.1
  101.5 0.7 fusion.18
  102.1 9.8 %custom-call.8 = f32[1,128,128]{1,2,0:T(8,128)S(1)} custom-call(f32[1,128,128]{2,1,0:T(8,128)S(1)} %fusion.18), custom_call_target="InvertDiagBlocksLowerTriangular" | custom-call | tf_op jit(solution)/shard_map/jit(_cho_solve)/triangular_solve | solution.py:12
  111.9 0.3 fusion.16
  112.4 1.1 multiply_reduce_fusion
  113.6 39.4 %psum.37 = f32[128]{0:T(128)S(1)} all-reduce(f32[128]{0:T(128)S(1)} %get-tuple-element.10), channel_id=1, replica_groups=mesh['row'=8,'col'=4] {'row','col'}, use_global_device_ids=true, to_apply=%region_5.0 | all-reduce | flops 128 | bytes 1024 | tf_op jit(solution)/shard_map/psum | solution.py:41
  153.0 10.2 %all_gather.7 = f32[512,128]{1,0:T(8,128)S(1)} all-gather(f32[128,128]{1,0:T(8,128)S(1)} %broadcast_divide_fusion), channel_id=1, replica_groups=mesh['row'=8,'col'=4] {'col'}, dimensions={0}, use_global_device_ids=true | all-gather | bytes 327680 | tf_op jit(solution)/shard_map/all_gather | solution.py:43
  163.2 1.2 fusion.36
  164.4 11.5 %fusion.11 = f32[512,128]{0,1:T(8,128)} fusion(f32[12,512,512]{2,1,0:T(8,128)} %param.6, f32[512,128]{1,0:T(8,128)S(1)} %all_gather.7, f32[12,128]{1,0:T(8,128)S(1)} %copy-done.1), kind=kOutput, calls=%fused_computation.9 | convolution fusion | flops 4832624640 | bytes 13113344 | tf_op jit(solution)/shard_map/kij,kir->jr/dot_general | solution.py:46
  175.9 54.6 %all-reduce.5.cloned.1.call-done = (f32[128,128]{0,1:T(8,128)}, f32[512,128]{0,1:T(8,128)}) async-done(((f32[128,128]{0,1:T(8,128)}, f32[512,128]{0,1:T(8,128)}), (f32[128,128]{0,1:T(8,128)}, f32[512,128]{0,1:T(8,128)})) %all-reduce.5.cloned.1.call-update) | async-done | bytes 327696 | tf_op jit(solution)/shard_map/psum | solution.py:48
  230.5 0.8 mul.48
  231.5 11.7 %cholesky.55 = f32[128,128]{1,0:T(8,128)S(1)} custom-call(f32[128,128]{1,0:T(8,128)S(1)} %fusion.23), custom_call_target="Cholesky" | custom-call | tf_op jit(solution)/shard_map/jit(cholesky)/cholesky | solution.py:11
  243.2 0.6 compare_reduce_fusion
  243.9 0.7 fusion.19
  244.5 9.8 %custom-call.9 = f32[1,128,128]{1,2,0:T(8,128)S(1)} custom-call(f32[1,128,128]{2,1,0:T(8,128)S(1)} %fusion.19), custom_call_target="InvertDiagBlocksLowerTriangular" | custom-call | tf_op jit(solution)/shard_map/jit(_cho_solve)/triangular_solve | solution.py:12
  254.3 0.3 fusion.14
  254.8 1.8 fusion.28
  (17 shorter events, 0.8 us)
Async XLA Ops:
  7.2 80.6 %all-reduce.7.cloned.1.call-start = ((), (), s32[]{:S(2)}) async-start(), calls=%async_computation.1 | async-start | bytes 655360 | tf_op jit(solution)/shard_map/psum | solution.py:37
  24.5 63.3 %copy-start.1 = (f32[12,128]{1,0:T(8,128)S(1)}, f32[12,128]{1,0:T(8,128)}, u32[]{:S(2)}) copy-start(f32[12,128]{1,0:T(8,128)} %param.8) | copy-start | bytes 18436
  42.9 187.6 %all-reduce.5.cloned.1.call-start = ((), (), s32[]{:S(2)}) async-start(), calls=%async_computation | async-start | bytes 655360 | tf_op jit(solution)/shard_map/psum | solution.py:48
  113.6 62.3 %copy-start = (f32[128,128]{1,0:T(8,128)}, f32[128,128]{1,0:T(8,128)S(1)}, u32[]{:S(2)}) copy-start(f32[128,128]{1,0:T(8,128)S(1)} %get-tuple-element.11) | copy-start | bytes 196612
Sparse Core Ops, SparseCore 0:
  43.0 44.7 all-reduce.6
  176.0 54.4 all-reduce.4
where the time goes:
time: 264 us; the launch traced here: 263 us
  waiting for transfers between devices  99.3 us (38%)
  blocking collectives  65.7 us (25%)
  other arithmetic  46.6 us (18%)
  matrix products  37.3 us (14%)
  between operations  14.2 us (5%)
    psum x1, waiting for transfers between devices, per_device(): gram_a = lax.psum(gram_piece, 'row')  54.6 us
    psum x1, waiting for transfers between devices, per_device(): gram_b = lax.psum(gram_part, 'col')  44.7 us
    psum x1, blocking collectives, per_device(): squares = lax.psum(jnp.sum(a_update * a_update, axis=0), ('row', 'col'))  39.4 us
    another operation x6, other arithmetic, solve_system(): lower = jnp.linalg.cholesky(system)  24.8 us
    another operation x4, other arithmetic, solve_system(): jax.scipy.linalg.cho_solve((lower, True), jnp.eye(system.shape[0], dtype=...  20.9 us
    dot_general x1, matrix products, per_device(): partial_a = jnp.einsum('kij,kjr->ir', block, khatri, precision=highest)  18.3 us
    all_gather x1, blocking collectives, per_device(): piece = lax.all_gather(factor_b, 'row', axis=0, tiled=True)  16.1 us
    dot_general x1, matrix products, per_device(): jnp.einsum('kij,kir->jr', block, khatri, precision=highest)  11.5 us
  transfers between devices with their start and end apart: 2, of which 2 were waited for; matrix products, arithmetic and copies ran while one was open for 0% of the time, Pallas kernels for 0%

commit v1 on v0

v1 whole, which is shorter than its diff:
```python
import functools

import jax
import jax.numpy as jnp
from jax import lax
from jax.experimental import pallas as pl
from jax.experimental.pallas import tpu as pltpu
from jax.sharding import PartitionSpec as P

EPSILON = 1e-06
MESH = pl.DeviceIdType.MESH
HIGHEST = lax.Precision.HIGHEST
PANEL = 8


def exact_dot(left, right):
    return jnp.dot(left, right, precision=HIGHEST, preferred_element_type=jnp.float32)


def fast_dot(left, right):
    return jnp.dot(left, right, preferred_element_type=jnp.float32)


def split(value):
    high = value.astype(jnp.bfloat16)
    low = (value - high.astype(jnp.float32)).astype(jnp.bfloat16)
    return high, low


def negative_inverse(system):
    size = system.shape[0]
    lane = lax.broadcasted_iota(jnp.int32, (PANEL, size), 1)
    sublane = lax.broadcasted_iota(jnp.int32, (PANEL, size), 0)
    whole_lane = lax.broadcasted_iota(jnp.int32, (size, size), 1)
    for base in range(0, size, PANEL):
        rows = system[base : base + PANEL, :]
        inside = (lane >= base) & (lane < base + PANEL)
        solved = jnp.where(inside, jnp.where(lane - base == sublane, -1.0, 0.0), rows)
        columns = jnp.stack(
            [jnp.broadcast_to(rows[:, base + t : base + t + 1], rows.shape) for t in range(PANEL)]
        )
        for t in range(PANEL):
            here = sublane == t
            column = columns[0]
            scale = 1.0 / jnp.broadcast_to(column[t : t + 1, :], rows.shape)
            factor = jnp.where(here, -1.0, column) * scale
            solved = jnp.where(here, 0.0, solved) - factor * solved[t : t + 1, :]
            if t < PANEL - 1:
                rest = columns[1:]
                columns = (
                    jnp.where(here[None], 0.0, rest) - factor[None] * rest[:, t : t + 1, :]
                )
        outside = (whole_lane < base) | (whole_lane >= base + PANEL)
        swept = jnp.where(outside, system, 0.0)
        for t in range(PANEL):
            swept = swept - system[:, base + t : base + t + 1] * solved[t : t + 1, :]
        pieces = [swept[:base], solved, swept[base + PANEL :]]
        system = jnp.concatenate([piece for piece in pieces if piece.shape[0]], axis=0)
    return system


def kernel(
    row_size, col_size,
    tensor, factor_b, factor_c,
    a_out, b_out,
    raw, high, low, piece, c_pad, grams, part_a, recv_a, a_all,
    gram_part, gram_recv, gram_all, acc_b, part_b, recv_b,
    load_sem, piece_send, piece_recv, gramb_send, gramb_recv,
    parta_send, parta_recv, a_send, a_recv,
    gs_send, gs_recv, gg_send, gg_recv, partb_send, partb_recv,
):
    depth, rows, cols = raw.shape
    rank = piece.shape[1]
    own_piece = factor_b.shape[0]
    own_a = rows // col_size
    own_b = cols // row_size
    own_g = rank // row_size
    row = lax.axis_index("row")
    col = lax.axis_index("col")

    def row_peer(d):
        return lax.rem(row + d, row_size)

    def col_peer(d):
        return lax.rem(col + d, col_size)

    def block(index, size):
        return pl.ds(pl.multiple_of(index * size, size), size)

    def loads(k):
        return pltpu.make_async_copy(tensor.at[k], raw.at[k], load_sem.at[k])

    for k in range(depth):
        loads(k).start()

    barrier = pltpu.get_barrier_semaphore()
    for d in range(1, row_size):
        pl.semaphore_signal(barrier, inc=1, device_id=(row_peer(d), col), device_id_type=MESH)
    for d in range(1, col_size):
        pl.semaphore_signal(barrier, inc=1, device_id=(row, col_peer(d)), device_id_type=MESH)
    pl.semaphore_wait(barrier, row_size + col_size - 2)

    def to_row(d, source, target, send, recv):
        return pltpu.make_async_remote_copy(
            src_ref=source, dst_ref=target, send_sem=send.at[d - 1], recv_sem=recv.at[d - 1],
            device_id=(row_peer(d), col), device_id_type=MESH,
        )

    def to_col(d, source, target, send, recv):
        return pltpu.make_async_remote_copy(
            src_ref=source, dst_ref=target, send_sem=send.at[d - 1], recv_sem=recv.at[d - 1],
            device_id=(row, col_peer(d)), device_id_type=MESH,
        )

    def piece_copy(d, owner):
        return to_row(d, factor_b, piece.at[block(owner, own_piece)], piece_send, piece_recv)

    for d in range(1, row_size):
        piece_copy(d, row).start()
    piece[block(row, own_piece), :] = factor_b[...]

    step = 64
    for k in range(depth):
        loads(k).wait()

        def split_rows(index, carry):
            here = block(index, step)
            high[k, here, :], low[k, here, :] = split(raw[k, here, :])
            return carry

        lax.fori_loop(0, rows // step, split_rows, 0)

    c_pad[...] = jnp.zeros(c_pad.shape, jnp.float32)
    c_pad[:depth, :] = factor_c[...]
    c_rows = c_pad[...]
    c_cols = c_rows.T
    c_gram = c_cols[:, 0:1] * c_rows[0:1, :]
    for k in range(1, depth):
        c_gram = c_gram + c_cols[:, k : k + 1] * c_rows[k : k + 1, :]

    for d in range(1, row_size):
        piece_copy(d, row_peer(row_size - d)).wait_recv()

    whole = piece[...]
    grams[col] = exact_dot(whole.T, whole)

    def gramb_copy(d, owner):
        return to_col(d, grams.at[owner], grams.at[owner], gramb_send, gramb_recv)

    for d in range(1, col_size):
        gramb_copy(d, col).start()

    piece_high, piece_low = split(whole)
    both = jnp.concatenate([piece_high, piece_low], axis=1)

    def parta_copy(d, slot):
        return to_col(
            d, part_a.at[block(col_peer(d), own_a)], recv_a.at[slot], parta_send, parta_recv
        )

    group = 4 if depth % 4 == 0 else 1
    for d in list(range(1, col_size)) + [0]:
        owner = col_peer(d)
        here = block(owner, own_a)
        total = jnp.zeros((own_a, rank), jnp.float32)
        for first in range(0, depth, group):
            span = slice(first, first + group)
            flat = (group * own_a, cols)
            left = fast_dot(high[span, here, :].reshape(flat), both)
            right = fast_dot(low[span, here, :].reshape(flat), piece_high)
            summed = left[:, :rank] + (left[:, rank:] + right)
            for k in range(group):
                total = total + summed[k * own_a : (k + 1) * own_a] * c_rows[first + k : first + k + 1, :]
        if d:
            part_a[here, :] = total
            parta_copy(d, d - 1).start()
        else:
            mine = total

    for d in range(1, col_size):
        gramb_copy(d, col_peer(col_size - d)).wait_recv()
    gram_b = grams[0]
    for index in range(1, col_size):
        gram_b = gram_b + grams[index]
    solve_a = negative_inverse(c_gram * gram_b)

    for d in range(1, col_size):
        parta_copy(d, d - 1).wait_recv()
        mine = mine + recv_a[d - 1]
    a_update = -exact_dot(mine, solve_a)
    a_out[...] = a_update
    a_all[block(col, own_a), :] = a_update

    def a_copy(d, owner):
        here = a_all.at[block(owner, own_a)]
        return to_col(d, here, here, a_send, a_recv)

    for d in range(1, col_size):
        a_copy(d, col).start()
    for d in range(1, col_size):
        a_copy(d, col_peer(col_size - d)).wait_recv()

    factor = a_all[...]
    turned = factor.T
    gram_part[...] = exact_dot(turned, factor)

    def gs_copy(d, slot):
        return to_row(
            d, gram_part.at[block(row_peer(d), own_g)], gram_recv.at[slot], gs_send, gs_recv
        )

    for d in range(1, row_size):
        gs_copy(d, d - 1).start()

    turned_high, turned_low = split(turned)
    stacked = jnp.concatenate([turned_high, turned_low], axis=0)

    def mode_two(k):
        left = fast_dot(stacked, high[k])
        right = fast_dot(turned_high, low[k])
        term = (left[:rank] + (left[rank:] + right)) * c_cols[:, k : k + 1]
        if k:
            acc_b[...] += term
        else:
            acc_b[...] = term

    half = depth // 2
    for k in range(half):
        mode_two(k)

    for d in range(1, row_size):
        gs_copy(d, d - 1).wait_recv()
    owned = gram_part[block(row, own_g), :]
    for d in range(1, row_size):
        owned = owned + gram_recv[d - 1]
    gram_all[block(row, own_g), :] = owned

    def gg_copy(d, owner):
        here = gram_all.at[block(owner, own_g)]
        return to_row(d, here, here, gg_send, gg_recv)

    for d in range(1, row_size):
        gg_copy(d, row).start()

    for k in range(half, depth):
        mode_two(k)
    part_b[...] = acc_b[...].T

    def partb_copy(d, slot):
        return to_row(
            d, part_b.at[block(row_peer(d), own_b)], recv_b.at[slot], partb_send, partb_recv
        )

    for d in range(1, row_size):
        partb_copy(d, d - 1).start()

    for d in range(1, row_size):
        gg_copy(d, row_peer(row_size - d)).wait_recv()
    gram_a = gram_all[...]
    diagonal = lax.broadcasted_iota(jnp.int32, (rank, rank), 0) == lax.broadcasted_iota(
        jnp.int32, (rank, rank), 1
    )
    squares = jnp.where(diagonal, gram_a, 0.0)
    inv_row = 1.0 / jnp.sqrt(jnp.sum(squares, axis=0, keepdims=True) + EPSILON)
    inv_col = 1.0 / jnp.sqrt(jnp.sum(squares, axis=1, keepdims=True) + EPSILON)
    solve_b = negative_inverse(c_gram * (gram_a * inv_row * inv_col))

    mine = part_b[block(row, own_b), :]
    for d in range(1, row_size):
        partb_copy(d, d - 1).wait_recv()
        mine = mine + recv_b[d - 1]
    b_out[...] = -exact_dot(mine * inv_row, solve_b)

    for d in range(1, row_size):
        piece_copy(d, row).wait_send()
        gs_copy(d, d - 1).wait_send()
        gg_copy(d, row).wait_send()
        partb_copy(d, d - 1).wait_send()
    for d in range(1, col_size):
        gramb_copy(d, col).wait_send()
        parta_copy(d, d - 1).wait_send()
        a_copy(d, col).wait_send()


def per_device(tensor, factor_b, factor_c):
    depth, rows, cols = tensor.shape
    rank = factor_c.shape[1]
    row_size, col_size = lax.axis_size("row"), lax.axis_size("col")
    own_a, own_b, own_g = rows // col_size, cols // row_size, rank // row_size
    f32, bf16 = jnp.float32, jnp.bfloat16
    vmem = pltpu.VMEM
    row_sem = pltpu.SemaphoreType.DMA((row_size - 1,))
    col_sem = pltpu.SemaphoreType.DMA((col_size - 1,))
    in_vmem = pl.BlockSpec(memory_space=pltpu.VMEM)
    return pl.pallas_call(
        functools.partial(kernel, row_size, col_size),
        out_shape=(
            jax.ShapeDtypeStruct((own_a, rank), f32),
            jax.ShapeDtypeStruct((own_b, rank), f32),
        ),
        in_specs=[pl.BlockSpec(memory_space=pl.ANY), in_vmem, in_vmem],
        out_specs=(in_vmem, in_vmem),
        scratch_shapes=[
            vmem((depth, rows, cols), f32),
            vmem((depth, rows, cols), bf16),
            vmem((depth, rows, cols), bf16),
            vmem((cols, rank), f32),
            vmem((rank, rank), f32),
            vmem((col_size, rank, rank), f32),
            vmem((rows, rank), f32),
            vmem((col_size - 1, own_a, rank), f32),
            vmem((rows, rank), f32),
            vmem((rank, rank), f32),
            vmem((row_size - 1, own_g, rank), f32),
            vmem((rank, rank), f32),
            vmem((rank, cols), f32),
            vmem((cols, rank), f32),
            vmem((row_size - 1, own_b, rank), f32),
            pltpu.SemaphoreType.DMA((depth,)),
            row_sem, row_sem,
            col_sem, col_sem,
            col_sem, col_sem,
            col_sem, col_sem,
            row_sem, row_sem,
            row_sem, row_sem,
            row_sem, row_sem,
        ],
        compiler_params=pltpu.CompilerParams(
            collective_id=0, has_side_effects=True, vmem_limit_bytes=52 * 1024 * 1024
        ),
        cost_estimate=pl.CostEstimate(
            flops=12 * depth * rows * cols * rank,
            bytes_accessed=4 * depth * rows * cols,
            transcendentals=0,
        ),
    )(tensor, factor_b, factor_c)


def solution(mesh):
    placed = (P(None, "row", "col"), P(("col", "row"), None), P())
    return jax.shard_map(
        per_device,
        mesh=mesh,
        in_specs=placed,
        out_specs=(P(("row", "col"), None), P(("col", "row"), None)),
        check_vma=False,
    )
```

time: 264 us -> 42.7 us (0.16)
  waiting for transfers between devices: 99.3 us -> 0 us
  blocking collectives: 65.7 us -> 0 us
  other arithmetic: 46.6 us -> 0 us
  Pallas kernels: 0 us -> 39 us
  matrix products: 37.3 us -> 0 us
  between operations: 14.2 us -> 0.65 us
    psum x2 -> x0, waiting for transfers between devices: 99.3 us -> none  [the longest x1 54.6 us: per_device(): gram_a = lax.psum(gram_piece, 'row')]
    another operation x10 -> x0, other arithmetic: 45.7 us -> none  [the longest x6 24.8 us: solve_system(): lower = jnp.linalg.cholesky(system)]
    psum x1 -> x0, blocking collectives: 39.4 us -> none  [per_device(): squares = lax.psum(jnp.sum(a_update * a_update, axis=0), ('row', 'col'))]
    pallas_call x0 -> x1, Pallas kernels: none -> 39 us  [per_device(): pl.pallas_call(functools.partial(kernel, row_size, col_size), out_shape=(...]
    dot_general x7 -> x0, matrix products: 36.3 us -> none  [the longest x1 18.3 us: per_device(): partial_a = jnp.einsum('kij,kjr->ir', block, khatri, precision=highest)]
    all_gather x2 -> x0, blocking collectives: 26.3 us -> none  [the longest x1 16.1 us: per_device(): piece = lax.all_gather(factor_b, 'row', axis=0, tiled=True)]
    unnamed x4 -> x6, local copies, waits for them, and re-layouts: 0.01 us -> 2.69 us
  transfers between devices with their start and end apart: 2 -> 0, of which waited for: 2 -> 0; matrix products, arithmetic and copies ran while one was open for 0% -> 0% of each run, Pallas kernels for 0% -> 0%
where the time goes in v1:
time: 42.7 us; the launch traced here: 42.4 us
  Pallas kernels  39 us (91%)
  local copies, waits for them, and re-layouts  2.69 us (6%)
  between operations  0.65 us (2%)
    pallas_call x1, Pallas kernels, per_device(): pl.pallas_call(functools.partial(kernel, row_size, col_size), out_shape=(...  39 us
    unnamed x6, local copies, waits for them, and re-layouts  2.69 us

profile of v1, /device:TPU:0, one launch (start us, length us, event | category | flops | bytes accessed | tf_op | source)
XLA Modules:
  0.0 42.4 jit_solution(3163203920052347377)
XLA Ops:
  0.6 0.0 copy-start
  0.6 0.7 %copy-done = f32[64,128]{1,0:T(8,128)S(1)} copy-done((f32[64,128]{1,0:T(8,128)S(1)}, f32[64,128]{1,0:T(8,128)}, u32[]{:S(2)}) %copy-start) | copy-done | bytes 32792
  1.4 0.0 copy-start.1
  1.4 0.7 %copy-done.1 = f32[12,128]{1,0:T(8,128)S(1)} copy-done((f32[12,128]{1,0:T(8,128)S(1)}, f32[12,128]{1,0:T(8,128)}, u32[]{:S(2)}) %copy-start.1) | copy-done | bytes 6168
  2.1 39.0 %shard_map.50 = (f32[128,128]{1,0:T(8,128)S(1)}, f32[64,128]{1,0:T(8,128)S(1)}) custom-call(f32[12,512,512]{2,1,0:T(8,128)} %tensor.1, f32[64,128]{1,0:T(8,128)S(1)} %copy-done, f32[12,128]{1,0:T(8,128)S(1)} %copy-done.1), custom_call_target="tpu_custom_call" | custom-call | flops 4831838208 | bytes 12582912 | tf_op jit(solution)/shard_map/pallas_call | solution.py:295
  41.1 0.6 %copy.7 = f32[128,128]{1,0:T(8,128)} copy(f32[128,128]{1,0:T(8,128)S(1)} %get-tuple-element.4) | data formatting | bytes 131072
  41.8 0.6 %copy.8 = f32[64,128]{1,0:T(8,128)} copy(f32[64,128]{1,0:T(8,128)S(1)} %get-tuple-element.5) | data formatting | bytes 65536
Async XLA Ops:
  0.6 0.8 %copy-start = (f32[64,128]{1,0:T(8,128)S(1)}, f32[64,128]{1,0:T(8,128)}, u32[]{:S(2)}) copy-start(f32[64,128]{1,0:T(8,128)} %factor_b.1) | copy-start | bytes 98308
  1.4 0.7 %copy-start.1 = (f32[12,128]{1,0:T(8,128)S(1)}, f32[12,128]{1,0:T(8,128)}, u32[]{:S(2)}) copy-start(f32[12,128]{1,0:T(8,128)} %factor_c.1) | copy-start | bytes 18436

commit v2 on v1

--- a/solution.py
+++ b/solution.py
@@ -27,36 +27,72 @@
     return high, low
 
 
+def reciprocal(value):
+    guess = pl.reciprocal(value, approx=True)
+    return guess * (2.0 - value * guess)
+
+
 def negative_inverse(system):
     size = system.shape[0]
-    lane = lax.broadcasted_iota(jnp.int32, (PANEL, size), 1)
-    sublane = lax.broadcasted_iota(jnp.int32, (PANEL, size), 0)
-    whole_lane = lax.broadcasted_iota(jnp.int32, (size, size), 1)
-    for base in range(0, size, PANEL):
-        rows = system[base : base + PANEL, :]
+    groups = size // PANEL
+    shape = (PANEL, size)
+    lane = lax.broadcasted_iota(jnp.int32, shape, 1)
+    sublane = lax.broadcasted_iota(jnp.int32, shape, 0)
+    whole_lane = lax.broadcasted_iota(jnp.int32, (groups, PANEL, size), 2)
+    diagonal = lax.broadcasted_iota(jnp.int32, (size, size), 0) == lax.broadcasted_iota(
+        jnp.int32, (size, size), 1
+    )
+    squares = jnp.where(diagonal, system, 0.0)
+    scales = lax.rsqrt(jnp.sum(squares, axis=0, keepdims=True)) * lax.rsqrt(
+        jnp.sum(squares, axis=1, keepdims=True)
+    )
+    system = (system * scales).reshape(groups, PANEL, size)
+    for panel in range(groups):
+        base = panel * PANEL
+        rows = system[panel]
         inside = (lane >= base) & (lane < base + PANEL)
-        solved = jnp.where(inside, jnp.where(lane - base == sublane, -1.0, 0.0), rows)
-        columns = jnp.stack(
-            [jnp.broadcast_to(rows[:, base + t : base + t + 1], rows.shape) for t in range(PANEL)]
-        )
-        for t in range(PANEL):
-            here = sublane == t
-            column = columns[0]
-            scale = 1.0 / jnp.broadcast_to(column[t : t + 1, :], rows.shape)
-            factor = jnp.where(here, -1.0, column) * scale
-            solved = jnp.where(here, 0.0, solved) - factor * solved[t : t + 1, :]
-            if t < PANEL - 1:
-                rest = columns[1:]
-                columns = (
-                    jnp.where(here[None], 0.0, rest) - factor[None] * rest[:, t : t + 1, :]
-                )
+        target = jnp.where(inside, jnp.where(lane - base == sublane, -1.0, 0.0), rows)
+        stack = jnp.stack(
+            [jnp.broadcast_to(rows[:, base + t : base + t + 1], shape) for t in range(PANEL)]
+            + [target]
+        )
+        grid = jnp.stack(
+            [jnp.broadcast_to(stack[:, i : i + 1, :], stack.shape) for i in range(PANEL)]
+        )
+        for t in range(0, PANEL, 2):
+            first, second, rest = grid[:, 0], grid[:, 1], grid[:, 2:]
+            one, both, two = first[t], second[t], second[t + 1]
+            scale = reciprocal(one * two - both * both)
+            upper = (two[None] * rest[t] - both[None] * rest[t + 1]) * scale[None]
+            lower = (one[None] * rest[t + 1] - both[None] * rest[t]) * scale[None]
+            pieces = []
+            for begin, end in ((0, t), (t + 2, PANEL)):
+                if begin < end:
+                    pieces.append(
+                        rest[begin:end]
+                        - (
+                            first[begin:end, None] * upper[None]
+                            + second[begin:end, None] * lower[None]
+                        )
+                    )
+                if begin == 0:
+                    pieces += [upper[None], lower[None]]
+            grid = jnp.concatenate(pieces, axis=0)
+        solved = grid[:, 0]
         outside = (whole_lane < base) | (whole_lane >= base + PANEL)
         swept = jnp.where(outside, system, 0.0)
-        for t in range(PANEL):
-            swept = swept - system[:, base + t : base + t + 1] * solved[t : t + 1, :]
-        pieces = [swept[:base], solved, swept[base + PANEL :]]
-        system = jnp.concatenate([piece for piece in pieces if piece.shape[0]], axis=0)
-    return system
+        terms = [
+            system[:, :, base + t : base + t + 1] * solved[t][None] for t in range(PANEL)
+        ]
+        while len(terms) > 1:
+            terms = [terms[i] + terms[i + 1] for i in range(0, len(terms), 2)]
+        swept = swept - terms[0]
+        own = solved[0]
+        for t in range(1, PANEL):
+            own = jnp.where(sublane == t, solved[t], own)
+        parts = [swept[:panel], own[None], swept[panel + 1 :]]
+        system = jnp.concatenate([part for part in parts if part.shape[0]], axis=0)
+    return system.reshape(size, size) * scales
 
 
 def kernel(
@@ -65,7 +101,7 @@
     a_out, b_out,
     raw, high, low, piece, c_pad, grams, part_a, recv_a, a_all,
     gram_part, gram_recv, gram_all, acc_b, part_b, recv_b,
-    load_sem, piece_send, piece_recv, gramb_send, gramb_recv,
+    load_sem, small_sem, piece_send, piece_recv, pair_send, pair_recv, gramb_send, gramb_recv,
     parta_send, parta_recv, a_send, a_recv,
     gs_send, gs_recv, gg_send, gg_recv, partb_send, partb_recv,
 ):
@@ -90,6 +126,13 @@
     def loads(k):
         return pltpu.make_async_copy(tensor.at[k], raw.at[k], load_sem.at[k])
 
+    piece_load = pltpu.make_async_copy(
+        factor_b, piece.at[block(row, own_piece)], small_sem.at[0]
+    )
+    c_load = pltpu.make_async_copy(factor_c, c_pad.at[pl.ds(0, depth)], small_sem.at[1])
+    c_pad[...] = jnp.zeros(c_pad.shape, jnp.float32)
+    piece_load.start()
+    c_load.start()
     for k in range(depth):
         loads(k).start()
 
@@ -112,12 +155,34 @@
             device_id=(row, col_peer(d)), device_id_type=MESH,
         )
 
+    pair = row + 1 - 2 * lax.rem(row, 2)
+    chips = row_size // 2
+
+    def chip_peer(d):
+        return lax.rem(row + 2 * d, row_size)
+
     def piece_copy(d, owner):
-        return to_row(d, factor_b, piece.at[block(owner, own_piece)], piece_send, piece_recv)
-
-    for d in range(1, row_size):
+        here = piece.at[block(owner, own_piece)]
+        return pltpu.make_async_remote_copy(
+            src_ref=here, dst_ref=here, send_sem=piece_send.at[d], recv_sem=piece_recv.at[d],
+            device_id=(chip_peer(d), col), device_id_type=MESH,
+        )
+
+    def pair_copy(d, owner):
+        here = piece.at[block(owner, own_piece)]
+        return pltpu.make_async_remote_copy(
+            src_ref=here, dst_ref=here, send_sem=pair_send.at[d], recv_sem=pair_recv.at[d],
+            device_id=(pair, col), device_id_type=MESH,
+        )
+
+    def partners(d):
+        owner = chip_peer(chips - d)
+        return owner + 1 - 2 * lax.rem(owner, 2)
+
+    piece_load.wait()
+    for d in range(1, chips):
         piece_copy(d, row).start()
-    piece[block(row, own_piece), :] = factor_b[...]
+    pair_copy(0, row).start()
 
     step = 64
     for k in range(depth):
@@ -130,16 +195,21 @@
 
         lax.fori_loop(0, rows // step, split_rows, 0)
 
-    c_pad[...] = jnp.zeros(c_pad.shape, jnp.float32)
-    c_pad[:depth, :] = factor_c[...]
+    for d in range(1, chips):
+        owner = chip_peer(chips - d)
+        piece_copy(d, owner).wait_recv()
+        pair_copy(d, owner).start()
+
+    c_load.wait()
     c_rows = c_pad[...]
     c_cols = c_rows.T
     c_gram = c_cols[:, 0:1] * c_rows[0:1, :]
     for k in range(1, depth):
         c_gram = c_gram + c_cols[:, k : k + 1] * c_rows[k : k + 1, :]
 
-    for d in range(1, row_size):
-        piece_copy(d, row_peer(row_size - d)).wait_recv()
+    pair_copy(0, pair).wait_recv()
+    for d in range(1, chips):
+        pair_copy(d, partners(d)).wait_recv()
 
     whole = piece[...]
     grams[col] = exact_dot(whole.T, whole)
@@ -162,6 +232,12 @@
     for d in list(range(1, col_size)) + [0]:
         owner = col_peer(d)
         here = block(owner, own_a)
+        if d == 0:
+            for other in range(1, col_size):
+                gramb_copy(other, col_peer(col_size - other)).wait_recv()
+            gram_b = grams[0]
+            for index in range(1, col_size):
+                gram_b = gram_b + grams[index]
         total = jnp.zeros((own_a, rank), jnp.float32)
         for first in range(0, depth, group):
             span = slice(first, first + group)
@@ -177,11 +253,6 @@
         else:
             mine = total
 
-    for d in range(1, col_size):
-        gramb_copy(d, col_peer(col_size - d)).wait_recv()
-    gram_b = grams[0]
-    for index in range(1, col_size):
-        gram_b = gram_b + grams[index]
     solve_a = negative_inverse(c_gram * gram_b)
 
     for d in range(1, col_size):
@@ -271,8 +342,11 @@
         mine = mine + recv_b[d - 1]
     b_out[...] = -exact_dot(mine * inv_row, solve_b)
 
-    for d in range(1, row_size):
+    pair_copy(0, row).wait_send()
+    for d in range(1, chips):
         piece_copy(d, row).wait_send()
+        pair_copy(d, chip_peer(chips - d)).wait_send()
+    for d in range(1, row_size):
         gs_copy(d, d - 1).wait_send()
         gg_copy(d, row).wait_send()
         partb_copy(d, d - 1).wait_send()
@@ -291,6 +365,7 @@
     vmem = pltpu.VMEM
     row_sem = pltpu.SemaphoreType.DMA((row_size - 1,))
     col_sem = pltpu.SemaphoreType.DMA((col_size - 1,))
+    chip_sem = pltpu.SemaphoreType.DMA((row_size // 2,))
     in_vmem = pl.BlockSpec(memory_space=pltpu.VMEM)
     return pl.pallas_call(
         functools.partial(kernel, row_size, col_size),
@@ -298,7 +373,7 @@
             jax.ShapeDtypeStruct((own_a, rank), f32),
             jax.ShapeDtypeStruct((own_b, rank), f32),
         ),
-        in_specs=[pl.BlockSpec(memory_space=pl.ANY), in_vmem, in_vmem],
+        in_specs=[pl.BlockSpec(memory_space=pl.ANY)] * 3,
         out_specs=(in_vmem, in_vmem),
         scratch_shapes=[
             vmem((depth, rows, cols), f32),
@@ -317,7 +392,8 @@
             vmem((cols, rank), f32),
             vmem((row_size - 1, own_b, rank), f32),
             pltpu.SemaphoreType.DMA((depth,)),
-            row_sem, row_sem,
+            pltpu.SemaphoreType.DMA((2,)),
+            chip_sem, chip_sem, chip_sem, chip_sem,
             col_sem, col_sem,
             col_sem, col_sem,
             col_sem, col_sem,
@@ -326,7 +402,7 @@
             row_sem, row_sem,
         ],
         compiler_params=pltpu.CompilerParams(
-            collective_id=0, has_side_effects=True, vmem_limit_bytes=52 * 1024 * 1024
+            collective_id=0, has_side_effects=True, vmem_limit_bytes=60 * 1024 * 1024
         ),
         cost_estimate=pl.CostEstimate(
             flops=12 * depth * rows * cols * rank,

time: 42.7 us -> 44.9 us (1.052)
  Pallas kernels: 39 us -> 41.2 us
    pallas_call x1, Pallas kernels: 39 us -> 41.2 us  [per_device(): pl.pallas_call(functools.partial(kernel, row_size, col_size), out_shape=(...]
    unnamed x6 -> x2, local copies, waits for them, and re-layouts: 2.69 us -> 2.85 us
where the time goes in v2:
time: 44.9 us; the launch traced here: 44.7 us
  Pallas kernels  41.2 us (92%)
  local copies, waits for them, and re-layouts  2.85 us (6%)
  between operations  0.64 us (1%)
    pallas_call x1, Pallas kernels, per_device(): pl.pallas_call(functools.partial(kernel, row_size, col_size), out_shape=(...  41.2 us
    unnamed x2, local copies, waits for them, and re-layouts  2.85 us

profile of v2, /device:TPU:0, one launch (start us, length us, event | category | flops | bytes accessed | tf_op | source)
XLA Modules:
  0.0 44.7 jit_solution(7256425115881498456)
XLA Ops:
  0.6 41.2 %shard_map.50 = (f32[128,128]{1,0:T(8,128)}, f32[64,128]{1,0:T(8,128)}) custom-call(f32[12,512,512]{2,1,0:T(8,128)} %tensor.1, f32[64,128]{1,0:T(8,128)} %factor_b.1, f32[12,128]{1,0:T(8,128)} %factor_c.1), custom_call_target="tpu_custom_call" | custom-call | flops 4831838208 | bytes 12582912 | tf_op jit(solution)/shard_map/pallas_call | solution.py:370
  41.9 1.5 %copy.7 = f32[128,128]{1,0:T(8,128)} copy(f32[128,128]{1,0:T(8,128)} %get-tuple-element.4) | data formatting | bytes 131072
  43.3 1.4 %copy.8 = f32[64,128]{1,0:T(8,128)} copy(f32[64,128]{1,0:T(8,128)} %get-tuple-element.5) | data formatting | bytes 65536

commit v3 on v2

--- a/solution.py
+++ b/solution.py
@@ -30,6 +30,23 @@
 def reciprocal(value):
     guess = pl.reciprocal(value, approx=True)
     return guess * (2.0 - value * guess)
+
+
+def thirds(value):
+    high = value.astype(jnp.bfloat16).astype(jnp.float32)
+    rest = value - high
+    middle = rest.astype(jnp.bfloat16).astype(jnp.float32)
+    return high, middle, rest - middle
+
+
+def outer_product(left, right):
+    l0, l1, l2 = thirds(left)
+    r0, r1, r2 = thirds(right)
+    lefts = jnp.concatenate([l0, l0, l1, l0, l1, l2], axis=0).astype(jnp.bfloat16)
+    rights = jnp.concatenate([r0, r1, r0, r2, r1, r0], axis=0).astype(jnp.bfloat16)
+    return lax.dot_general(
+        lefts, rights, (((0,), (0,)), ((), ())), preferred_element_type=jnp.float32
+    )
 
 
 def negative_inverse(system):
@@ -79,18 +96,24 @@
                     pieces += [upper[None], lower[None]]
             grid = jnp.concatenate(pieces, axis=0)
         solved = grid[:, 0]
-        outside = (whole_lane < base) | (whole_lane >= base + PANEL)
-        swept = jnp.where(outside, system, 0.0)
-        terms = [
-            system[:, :, base + t : base + t + 1] * solved[t][None] for t in range(PANEL)
-        ]
-        while len(terms) > 1:
-            terms = [terms[i] + terms[i + 1] for i in range(0, len(terms), 2)]
-        swept = swept - terms[0]
         own = solved[0]
         for t in range(1, PANEL):
             own = jnp.where(sublane == t, solved[t], own)
-        parts = [swept[:panel], own[None], swept[panel + 1 :]]
+        if panel + 1 < groups:
+            after = system[panel + 1]
+            terms = [
+                jnp.broadcast_to(after[:, base + t : base + t + 1], shape) * solved[t]
+                for t in range(PANEL)
+            ]
+            while len(terms) > 1:
+                terms = [terms[i] + terms[i + 1] for i in range(0, len(terms), 2)]
+            ahead = jnp.where(inside, 0.0, after) - terms[0]
+        outside = (whole_lane < base) | (whole_lane >= base + PANEL)
+        product = outer_product(rows, own).reshape(groups, PANEL, size)
+        swept = jnp.where(outside, system, 0.0) - product
+        parts = [swept[:panel], own[None]]
+        if panel + 1 < groups:
+            parts += [ahead[None], swept[panel + 2 :]]
         system = jnp.concatenate([part for part in parts if part.shape[0]], axis=0)
     return system.reshape(size, size) * scales
 
@@ -356,6 +379,17 @@
         a_copy(d, col).wait_send()
 
 
+def finish(a_update, b_update, a_out, b_out, sems):
+    copies = [
+        pltpu.make_async_copy(a_update, a_out, sems.at[0]),
+        pltpu.make_async_copy(b_update, b_out, sems.at[1]),
+    ]
+    for copy in copies:
+        copy.start()
+    for copy in copies:
+        copy.wait()
+
+
 def per_device(tensor, factor_b, factor_c):
     depth, rows, cols = tensor.shape
     rank = factor_c.shape[1]
@@ -367,13 +401,14 @@
     col_sem = pltpu.SemaphoreType.DMA((col_size - 1,))
     chip_sem = pltpu.SemaphoreType.DMA((row_size // 2,))
     in_vmem = pl.BlockSpec(memory_space=pltpu.VMEM)
-    return pl.pallas_call(
+    shapes = (
+        jax.ShapeDtypeStruct((own_a, rank), f32),
+        jax.ShapeDtypeStruct((own_b, rank), f32),
+    )
+    updates = pl.pallas_call(
         functools.partial(kernel, row_size, col_size),
-        out_shape=(
-            jax.ShapeDtypeStruct((own_a, rank), f32),
-            jax.ShapeDtypeStruct((own_b, rank), f32),
-        ),
-        in_specs=[pl.BlockSpec(memory_space=pl.ANY)] * 3,
+        out_shape=shapes,
+        in_specs=[pl.BlockSpec(memory_space=pltpu.HBM)] * 3,
         out_specs=(in_vmem, in_vmem),
         scratch_shapes=[
             vmem((depth, rows, cols), f32),
@@ -402,7 +437,7 @@
             row_sem, row_sem,
         ],
         compiler_params=pltpu.CompilerParams(
-            collective_id=0, has_side_effects=True, vmem_limit_bytes=60 * 1024 * 1024
+            collective_id=0, has_side_effects=True, vmem_limit_bytes=52 * 1024 * 1024
         ),
         cost_estimate=pl.CostEstimate(
             flops=12 * depth * rows * cols * rank,
@@ -410,6 +445,15 @@
             transcendentals=0,
         ),
     )(tensor, factor_b, factor_c)
+    anywhere = pl.BlockSpec(memory_space=pl.ANY)
+    return pl.pallas_call(
+        finish,
+        out_shape=shapes,
+        in_specs=[anywhere] * 2,
+        out_specs=(anywhere, anywhere),
+        scratch_shapes=[pltpu.SemaphoreType.DMA((2,))],
+        compiler_params=pltpu.CompilerParams(vmem_limit_bytes=1024 * 1024),
+    )(*updates)
 
 
 def solution(mesh):

time: 44.9 us -> 41.7 us (0.929)
  Pallas kernels: 41.2 us -> 39.3 us
  local copies, waits for them, and re-layouts: 2.85 us -> 1.45 us
    pallas_call x1 -> x2, Pallas kernels: 41.2 us -> 39.3 us  [the longest x1 38.6 us: per_device(): pl.pallas_call(functools.partial(kernel, row_size, col_size), out_shape=s...]
    unnamed x2 -> x4, local copies, waits for them, and re-layouts: 2.85 us -> 1.45 us
where the time goes in v3:
time: 41.7 us; the launch traced here: 41.4 us
  Pallas kernels  39.3 us (94%)
  local copies, waits for them, and re-layouts  1.45 us (3%)
  between operations  0.65 us (2%)
    pallas_call x1, Pallas kernels, per_device(): pl.pallas_call(functools.partial(kernel, row_size, col_size), out_shape=s...  38.6 us
    unnamed x4, local copies, waits for them, and re-layouts  1.45 us

profile of v3, /device:TPU:0, one launch (start us, length us, event | category | flops | bytes accessed | tf_op | source)
XLA Modules:
  0.0 41.4 jit_solution(6260295293862081717)
XLA Ops:
  0.6 0.0 copy-start
  0.6 0.7 %copy-done = f32[64,128]{1,0:T(8,128)S(1)} copy-done((f32[64,128]{1,0:T(8,128)S(1)}, f32[64,128]{1,0:T(8,128)}, u32[]{:S(2)}) %copy-start) | copy-done | bytes 32792
  1.4 0.0 copy-start.1
  1.4 0.7 %copy-done.1 = f32[12,128]{1,0:T(8,128)S(1)} copy-done((f32[12,128]{1,0:T(8,128)S(1)}, f32[12,128]{1,0:T(8,128)}, u32[]{:S(2)}) %copy-start.1) | copy-done | bytes 6168
  2.1 38.6 %shard_map.50 = (f32[128,128]{1,0:T(8,128)S(1)}, f32[64,128]{1,0:T(8,128)S(1)}) custom-call(f32[12,512,512]{2,1,0:T(8,128)} %tensor.1, f32[64,128]{1,0:T(8,128)S(1)} %copy-done, f32[12,128]{1,0:T(8,128)S(1)} %copy-done.1), custom_call_target="tpu_custom_call" | custom-call | flops 4831838208 | bytes 12582912 | tf_op jit(solution)/shard_map/pallas_call | solution.py:408
  40.7 0.7 %shard_map.51 = (f32[128,128]{1,0:T(8,128)}, f32[64,128]{1,0:T(8,128)}) custom-call(f32[128,128]{1,0:T(8,128)S(1)} %get-tuple-element.4.a_update, f32[64,128]{1,0:T(8,128)S(1)} %get-tuple-element.5.b_update), custom_call_target="tpu_custom_call" | custom-call | tf_op jit(solution)/shard_map/pallas_call | solution.py:449
Async XLA Ops:
  0.6 0.8 %copy-start = (f32[64,128]{1,0:T(8,128)S(1)}, f32[64,128]{1,0:T(8,128)}, u32[]{:S(2)}) copy-start(f32[64,128]{1,0:T(8,128)} %factor_b.1) | copy-start | bytes 98308
  1.4 0.7 %copy-start.1 = (f32[12,128]{1,0:T(8,128)S(1)}, f32[12,128]{1,0:T(8,128)}, u32[]{:S(2)}) copy-start(f32[12,128]{1,0:T(8,128)} %factor_c.1) | copy-start | bytes 18436

commit v4 on v3

--- a/solution.py
+++ b/solution.py
@@ -49,7 +49,7 @@
     )
 
 
-def negative_inverse(system):
+def negative_inverse(system, beside=None):
     size = system.shape[0]
     groups = size // PANEL
     shape = (PANEL, size)
@@ -115,6 +115,8 @@
         if panel + 1 < groups:
             parts += [ahead[None], swept[panel + 2 :]]
         system = jnp.concatenate([part for part in parts if part.shape[0]], axis=0)
+        if beside is not None:
+            beside(panel)
     return system.reshape(size, size) * scales
 
 
@@ -252,32 +254,45 @@
         )
 
     group = 4 if depth % 4 == 0 else 1
-    for d in list(range(1, col_size)) + [0]:
+    state = {}
+
+    def mode_one(d, first):
         owner = col_peer(d)
         here = block(owner, own_a)
-        if d == 0:
-            for other in range(1, col_size):
-                gramb_copy(other, col_peer(col_size - other)).wait_recv()
-            gram_b = grams[0]
-            for index in range(1, col_size):
-                gram_b = gram_b + grams[index]
-        total = jnp.zeros((own_a, rank), jnp.float32)
-        for first in range(0, depth, group):
-            span = slice(first, first + group)
-            flat = (group * own_a, cols)
-            left = fast_dot(high[span, here, :].reshape(flat), both)
-            right = fast_dot(low[span, here, :].reshape(flat), piece_high)
-            summed = left[:, :rank] + (left[:, rank:] + right)
-            for k in range(group):
-                total = total + summed[k * own_a : (k + 1) * own_a] * c_rows[first + k : first + k + 1, :]
-        if d:
+        span = slice(first, first + group)
+        flat = (group * own_a, cols)
+        left = fast_dot(high[span, here, :].reshape(flat), both)
+        right = fast_dot(low[span, here, :].reshape(flat), piece_high)
+        summed = left[:, :rank] + (left[:, rank:] + right)
+        total = state["total"] if first else 0.0
+        for k in range(group):
+            total = total + summed[k * own_a : (k + 1) * own_a] * c_rows[first + k : first + k + 1, :]
+        state["total"] = total
+        if first + group == depth and d:
             part_a[here, :] = total
             parta_copy(d, d - 1).start()
-        else:
-            mine = total
-
-    solve_a = negative_inverse(c_gram * gram_b)
-
+
+    order = list(range(1, col_size)) + [0]
+    items = [(d, first) for d in order for first in range(0, depth, group)]
+    lead = len(items) * 5 // 12
+    for item in items[:lead]:
+        mode_one(*item)
+    items = items[lead:]
+    panels = rank // PANEL
+    share = -(-len(items) // (panels // 2))
+
+    def beside_a(panel):
+        for item in items[panel * share : (panel + 1) * share]:
+            mode_one(*item)
+
+    for d in range(1, col_size):
+        gramb_copy(d, col_peer(col_size - d)).wait_recv()
+    gram_b = grams[0]
+    for index in range(1, col_size):
+        gram_b = gram_b + grams[index]
+    solve_a = negative_inverse(c_gram * gram_b, beside_a)
+
+    mine = state["total"]
     for d in range(1, col_size):
         parta_copy(d, d - 1).wait_recv()
         mine = mine + recv_a[d - 1]
@@ -309,18 +324,37 @@
     turned_high, turned_low = split(turned)
     stacked = jnp.concatenate([turned_high, turned_low], axis=0)
 
-    def mode_two(k):
-        left = fast_dot(stacked, high[k])
-        right = fast_dot(turned_high, low[k])
+    width = cols // 2
+
+    def mode_two(k, half):
+        lanes = slice(half * width, (half + 1) * width)
+        left = fast_dot(stacked, high[k, :, lanes])
+        right = fast_dot(turned_high, low[k, :, lanes])
         term = (left[:rank] + (left[rank:] + right)) * c_cols[:, k : k + 1]
         if k:
-            acc_b[...] += term
+            acc_b[half] += term
         else:
-            acc_b[...] = term
-
-    half = depth // 2
-    for k in range(half):
-        mode_two(k)
+            acc_b[half] = term
+
+    def partb_copy(owner, slot):
+        d = lax.rem(owner - row + row_size, row_size)
+        return pltpu.make_async_remote_copy(
+            src_ref=part_b.at[block(owner, own_b)], dst_ref=recv_b.at[slot],
+            send_sem=partb_send.at[d - 1], recv_sem=partb_recv.at[d - 1],
+            device_id=(owner, col), device_id_type=MESH,
+        )
+
+    def send_half(half):
+        part_b[half * width : (half + 1) * width, :] = acc_b[half].T
+        for owner in range(half * row_size // 2, (half + 1) * row_size // 2):
+
+            @pl.when(row != owner)
+            def _():
+                partb_copy(owner, lax.rem(owner - row + row_size, row_size) - 1).start()
+
+    early = 2 * depth // 3
+    for k in range(early):
+        mode_two(k, 0)
 
     for d in range(1, row_size):
         gs_copy(d, d - 1).wait_recv()
@@ -336,17 +370,18 @@
     for d in range(1, row_size):
         gg_copy(d, row).start()
 
-    for k in range(half, depth):
-        mode_two(k)
-    part_b[...] = acc_b[...].T
-
-    def partb_copy(d, slot):
-        return to_row(
-            d, part_b.at[block(row_peer(d), own_b)], recv_b.at[slot], partb_send, partb_recv
-        )
-
-    for d in range(1, row_size):
-        partb_copy(d, d - 1).start()
+    for k in range(early, depth):
+        mode_two(k, 0)
+    send_half(0)
+    for k in range(depth // 2):
+        mode_two(k, 1)
+
+    def beside_b(panel):
+        k = depth // 2 + panel
+        if k < depth:
+            mode_two(k, 1)
+            if k == depth - 1:
+                send_half(1)
 
     for d in range(1, row_size):
         gg_copy(d, row_peer(row_size - d)).wait_recv()
@@ -357,11 +392,11 @@
     squares = jnp.where(diagonal, gram_a, 0.0)
     inv_row = 1.0 / jnp.sqrt(jnp.sum(squares, axis=0, keepdims=True) + EPSILON)
     inv_col = 1.0 / jnp.sqrt(jnp.sum(squares, axis=1, keepdims=True) + EPSILON)
-    solve_b = negative_inverse(c_gram * (gram_a * inv_row * inv_col))
+    solve_b = negative_inverse(c_gram * (gram_a * inv_row * inv_col), beside_b)
 
     mine = part_b[block(row, own_b), :]
     for d in range(1, row_size):
-        partb_copy(d, d - 1).wait_recv()
+        partb_copy(row_peer(d), d - 1).wait_recv()
         mine = mine + recv_b[d - 1]
     b_out[...] = -exact_dot(mine * inv_row, solve_b)
 
@@ -372,7 +407,7 @@
     for d in range(1, row_size):
         gs_copy(d, d - 1).wait_send()
         gg_copy(d, row).wait_send()
-        partb_copy(d, d - 1).wait_send()
+        partb_copy(row_peer(d), d - 1).wait_send()
     for d in range(1, col_size):
         gramb_copy(d, col).wait_send()
         parta_copy(d, d - 1).wait_send()
@@ -423,7 +458,7 @@
             vmem((rank, rank), f32),
             vmem((row_size - 1, own_g, rank), f32),
             vmem((rank, rank), f32),
-            vmem((rank, cols), f32),
+            vmem((2, rank, cols // 2), f32),
             vmem((cols, rank), f32),
             vmem((row_size - 1, own_b, rank), f32),
             pltpu.SemaphoreType.DMA((depth,)),

time: 41.7 us -> 49.7 us (1.19)
  the two profiles are of different devices: /device:TPU:0 before, /device:TPU:25 now
where the time goes in v4:
time: 49.7 us; the launch traced here: 49.5 us
  Pallas kernels  47.4 us (95%)
  local copies, waits for them, and re-layouts  1.45 us (3%)
  between operations  0.65 us (1%)
    pallas_call x1, Pallas kernels, per_device(): pl.pallas_call(functools.partial(kernel, row_size, col_size), out_shape=s...  46.8 us
    unnamed x4, local copies, waits for them, and re-layouts  1.45 us

profile of v4, /device:TPU:25, one launch (start us, length us, event | category | flops | bytes accessed | tf_op | source)
XLA Modules:
  0.0 49.5 jit_solution(66962550259663948)
XLA Ops:
  0.6 0.0 copy-start
  0.6 0.7 %copy-done = f32[64,128]{1,0:T(8,128)S(1)} copy-done((f32[64,128]{1,0:T(8,128)S(1)}, f32[64,128]{1,0:T(8,128)}, u32[]{:S(2)}) %copy-start) | copy-done | bytes 32792
  1.4 0.0 copy-start.1
  1.4 0.7 %copy-done.1 = f32[12,128]{1,0:T(8,128)S(1)} copy-done((f32[12,128]{1,0:T(8,128)S(1)}, f32[12,128]{1,0:T(8,128)}, u32[]{:S(2)}) %copy-start.1) | copy-done | bytes 6168
  2.1 46.8 %shard_map.50 = (f32[128,128]{1,0:T(8,128)S(1)}, f32[64,128]{1,0:T(8,128)S(1)}) custom-call(f32[12,512,512]{2,1,0:T(8,128)} %tensor.1, f32[64,128]{1,0:T(8,128)S(1)} %copy-done, f32[12,128]{1,0:T(8,128)S(1)} %copy-done.1), custom_call_target="tpu_custom_call" | custom-call | flops 4831838208 | bytes 12582912 | tf_op jit(solution)/shard_map/pallas_call | solution.py:443
  48.8 0.7 %shard_map.51 = (f32[128,128]{1,0:T(8,128)}, f32[64,128]{1,0:T(8,128)}) custom-call(f32[128,128]{1,0:T(8,128)S(1)} %get-tuple-element.4.a_update, f32[64,128]{1,0:T(8,128)S(1)} %get-tuple-element.5.b_update), custom_call_target="tpu_custom_call" | custom-call | tf_op jit(solution)/shard_map/pallas_call | solution.py:484
Async XLA Ops:
  0.6 0.8 %copy-start = (f32[64,128]{1,0:T(8,128)S(1)}, f32[64,128]{1,0:T(8,128)}, u32[]{:S(2)}) copy-start(f32[64,128]{1,0:T(8,128)} %factor_b.1) | copy-start | bytes 98308
  1.4 0.7 %copy-start.1 = (f32[12,128]{1,0:T(8,128)S(1)}, f32[12,128]{1,0:T(8,128)}, u32[]{:S(2)}) copy-start(f32[12,128]{1,0:T(8,128)} %factor_c.1) | copy-start | bytes 18436

commit v5 on v3

--- a/solution.py
+++ b/solution.py
@@ -73,36 +73,25 @@
             [jnp.broadcast_to(rows[:, base + t : base + t + 1], shape) for t in range(PANEL)]
             + [target]
         )
-        grid = jnp.stack(
-            [jnp.broadcast_to(stack[:, i : i + 1, :], stack.shape) for i in range(PANEL)]
-        )
         for t in range(0, PANEL, 2):
-            first, second, rest = grid[:, 0], grid[:, 1], grid[:, 2:]
-            one, both, two = first[t], second[t], second[t + 1]
+            first, second, rest = stack[0], stack[1], stack[2:]
+            one = jnp.broadcast_to(first[t : t + 1, :], shape)
+            both = jnp.broadcast_to(second[t : t + 1, :], shape)
+            two = jnp.broadcast_to(second[t + 1 : t + 2, :], shape)
+            upper, lower = sublane == t, sublane == t + 1
             scale = reciprocal(one * two - both * both)
-            upper = (two[None] * rest[t] - both[None] * rest[t + 1]) * scale[None]
-            lower = (one[None] * rest[t + 1] - both[None] * rest[t]) * scale[None]
-            pieces = []
-            for begin, end in ((0, t), (t + 2, PANEL)):
-                if begin < end:
-                    pieces.append(
-                        rest[begin:end]
-                        - (
-                            first[begin:end, None] * upper[None]
-                            + second[begin:end, None] * lower[None]
-                        )
-                    )
-                if begin == 0:
-                    pieces += [upper[None], lower[None]]
-            grid = jnp.concatenate(pieces, axis=0)
-        solved = grid[:, 0]
-        own = solved[0]
-        for t in range(1, PANEL):
-            own = jnp.where(sublane == t, solved[t], own)
+            left = jnp.where(upper, -two, jnp.where(lower, both, first * two - second * both))
+            right = jnp.where(upper, both, jnp.where(lower, -one, second * one - first * both))
+            left, right = left * scale, right * scale
+            kept = jnp.where((upper | lower)[None], 0.0, rest)
+            stack = kept - (
+                left[None] * rest[:, t : t + 1, :] + right[None] * rest[:, t + 1 : t + 2, :]
+            )
+        own = stack[0]
         if panel + 1 < groups:
             after = system[panel + 1]
             terms = [
-                jnp.broadcast_to(after[:, base + t : base + t + 1], shape) * solved[t]
+                jnp.broadcast_to(after[:, base + t : base + t + 1], shape) * own[t : t + 1, :]
                 for t in range(PANEL)
             ]
             while len(terms) > 1:
@@ -122,7 +111,7 @@
     row_size, col_size,
     tensor, factor_b, factor_c,
     a_out, b_out,
-    raw, high, low, piece, c_pad, grams, part_a, recv_a, a_all,
+    raw, parts, piece, c_pad, grams, part_a, recv_a, a_all,
     gram_part, gram_recv, gram_all, acc_b, part_b, recv_b,
     load_sem, small_sem, piece_send, piece_recv, pair_send, pair_recv, gramb_send, gramb_recv,
     parta_send, parta_recv, a_send, a_recv,
@@ -213,7 +202,7 @@
 
         def split_rows(index, carry):
             here = block(index, step)
-            high[k, here, :], low[k, here, :] = split(raw[k, here, :])
+            parts[k, here, :cols], parts[k, here, cols:] = split(raw[k, here, :])
             return carry
 
         lax.fori_loop(0, rows // step, split_rows, 0)
@@ -244,7 +233,13 @@
         gramb_copy(d, col).start()
 
     piece_high, piece_low = split(whole)
-    both = jnp.concatenate([piece_high, piece_low], axis=1)
+    both = jnp.concatenate(
+        [
+            jnp.concatenate([piece_high, piece_low], axis=1),
+            jnp.concatenate([piece_high, jnp.zeros_like(piece_low)], axis=1),
+        ],
+        axis=0,
+    )
 
     def parta_copy(d, slot):
         return to_col(
@@ -264,10 +259,8 @@
         total = jnp.zeros((own_a, rank), jnp.float32)
         for first in range(0, depth, group):
             span = slice(first, first + group)
-            flat = (group * own_a, cols)
-            left = fast_dot(high[span, here, :].reshape(flat), both)
-            right = fast_dot(low[span, here, :].reshape(flat), piece_high)
-            summed = left[:, :rank] + (left[:, rank:] + right)
+            product = fast_dot(parts[span, here, :].reshape(group * own_a, 2 * cols), both)
+            summed = product[:, :rank] + product[:, rank:]
             for k in range(group):
                 total = total + summed[k * own_a : (k + 1) * own_a] * c_rows[first + k : first + k + 1, :]
         if d:
@@ -310,8 +303,8 @@
     stacked = jnp.concatenate([turned_high, turned_low], axis=0)
 
     def mode_two(k):
-        left = fast_dot(stacked, high[k])
-        right = fast_dot(turned_high, low[k])
+        left = fast_dot(stacked, parts[k, :, :cols])
+        right = fast_dot(turned_high, parts[k, :, cols:])
         term = (left[:rank] + (left[rank:] + right)) * c_cols[:, k : k + 1]
         if k:
             acc_b[...] += term
@@ -412,8 +405,7 @@
         out_specs=(in_vmem, in_vmem),
         scratch_shapes=[
             vmem((depth, rows, cols), f32),
-            vmem((depth, rows, cols), bf16),
-            vmem((depth, rows, cols), bf16),
+            vmem((depth, rows, 2 * cols), bf16),
             vmem((cols, rank), f32),
             vmem((rank, rank), f32),
             vmem((col_size, rank, rank), f32),

time: 41.7 us -> 41.6 us (level)
  no operation moved by 1% of the time
where the time goes in v5:
time: 41.6 us; the launch traced here: 41.3 us
  Pallas kernels  39.2 us (94%)
  local copies, waits for them, and re-layouts  1.45 us (3%)
  between operations  0.65 us (2%)
    pallas_call x1, Pallas kernels, per_device(): pl.pallas_call(functools.partial(kernel, row_size, col_size), out_shape=s...  38.5 us
    unnamed x4, local copies, waits for them, and re-layouts  1.45 us

profile of v5, /device:TPU:0, one launch (start us, length us, event | category | flops | bytes accessed | tf_op | source)
XLA Modules:
  0.0 41.3 jit_solution(9923274511309304609)
XLA Ops:
  0.6 0.0 copy-start
  0.6 0.7 %copy-done = f32[64,128]{1,0:T(8,128)S(1)} copy-done((f32[64,128]{1,0:T(8,128)S(1)}, f32[64,128]{1,0:T(8,128)}, u32[]{:S(2)}) %copy-start) | copy-done | bytes 32792
  1.4 0.0 copy-start.1
  1.4 0.7 %copy-done.1 = f32[12,128]{1,0:T(8,128)S(1)} copy-done((f32[12,128]{1,0:T(8,128)S(1)}, f32[12,128]{1,0:T(8,128)}, u32[]{:S(2)}) %copy-start.1) | copy-done | bytes 6168
  2.1 38.5 %shard_map.50 = (f32[128,128]{1,0:T(8,128)S(1)}, f32[64,128]{1,0:T(8,128)S(1)}) custom-call(f32[12,512,512]{2,1,0:T(8,128)} %tensor.1, f32[64,128]{1,0:T(8,128)S(1)} %copy-done, f32[12,128]{1,0:T(8,128)S(1)} %copy-done.1), custom_call_target="tpu_custom_call" | custom-call | flops 4831838208 | bytes 12582912 | tf_op jit(solution)/shard_map/pallas_call | solution.py:401
  40.6 0.7 %shard_map.51 = (f32[128,128]{1,0:T(8,128)}, f32[64,128]{1,0:T(8,128)}) custom-call(f32[128,128]{1,0:T(8,128)S(1)} %get-tuple-element.4.a_update, f32[64,128]{1,0:T(8,128)S(1)} %get-tuple-element.5.b_update), custom_call_target="tpu_custom_call" | custom-call | tf_op jit(solution)/shard_map/pallas_call | solution.py:441
Async XLA Ops:
  0.6 0.8 %copy-start = (f32[64,128]{1,0:T(8,128)S(1)}, f32[64,128]{1,0:T(8,128)}, u32[]{:S(2)}) copy-start(f32[64,128]{1,0:T(8,128)} %factor_b.1) | copy-start | bytes 98308
  1.4 0.7 %copy-start.1 = (f32[12,128]{1,0:T(8,128)S(1)}, f32[12,128]{1,0:T(8,128)}, u32[]{:S(2)}) copy-start(f32[12,128]{1,0:T(8,128)} %factor_c.1) | copy-start | bytes 18436

commit v6 on v5

--- a/solution.py
+++ b/solution.py
@@ -49,7 +49,7 @@
     )
 
 
-def negative_inverse(system):
+def negative_inverse(system, beside=None):
     size = system.shape[0]
     groups = size // PANEL
     shape = (PANEL, size)
@@ -104,6 +104,8 @@
         if panel + 1 < groups:
             parts += [ahead[None], swept[panel + 2 :]]
         system = jnp.concatenate([part for part in parts if part.shape[0]], axis=0)
+        if beside is not None:
+            beside(panel)
     return system.reshape(size, size) * scales
 
 
@@ -112,10 +114,10 @@
     tensor, factor_b, factor_c,
     a_out, b_out,
     raw, parts, piece, c_pad, grams, part_a, recv_a, a_all,
-    gram_part, gram_recv, gram_all, acc_b, part_b, recv_b,
+    gram_part, gram_recv, gram_all, acc_b, part_b, half_b, sum_b, recv_b,
     load_sem, small_sem, piece_send, piece_recv, pair_send, pair_recv, gramb_send, gramb_recv,
     parta_send, parta_recv, a_send, a_recv,
-    gs_send, gs_recv, gg_send, gg_recv, partb_send, partb_recv,
+    gs_send, gs_recv, gg_send, gg_recv, half_sem, partb_send, partb_recv,
 ):
     depth, rows, cols = raw.shape
     rank = piece.shape[1]
@@ -331,15 +333,32 @@
 
     for k in range(half, depth):
         mode_two(k)
-    part_b[...] = acc_b[...].T
-
-    def partb_copy(d, slot):
-        return to_row(
-            d, part_b.at[block(row_peer(d), own_b)], recv_b.at[slot], partb_send, partb_recv
-        )
-
-    for d in range(1, row_size):
-        partb_copy(d, d - 1).start()
+    core = lax.rem(row, 2)
+    chip = lax.div(row, 2)
+    turned_b = acc_b[...].T
+    for owner in range(row_size):
+        spot = slice(owner // 2 * own_b, (owner // 2 + 1) * own_b)
+        part_b[owner % 2, spot, :] = turned_b[owner * own_b : (owner + 1) * own_b]
+
+    half_copy = pltpu.make_async_remote_copy(
+        src_ref=part_b.at[1 - core], dst_ref=half_b, send_sem=half_sem.at[0],
+        recv_sem=half_sem.at[1], device_id=(pair, col), device_id_type=MESH,
+    )
+    half_copy.start()
+
+    def partb_copy(d):
+        return pltpu.make_async_remote_copy(
+            src_ref=sum_b.at[block(lax.rem(chip + d, chips), own_b)], dst_ref=recv_b.at[d - 1],
+            send_sem=partb_send.at[d], recv_sem=partb_recv.at[d],
+            device_id=(chip_peer(d), col), device_id_type=MESH,
+        )
+
+    def beside_b(panel):
+        if panel == 3:
+            half_copy.wait_recv()
+            sum_b[...] = part_b[core] + half_b[...]
+            for d in range(1, chips):
+                partb_copy(d).start()
 
     for d in range(1, row_size):
         gg_copy(d, row_peer(row_size - d)).wait_recv()
@@ -350,22 +369,23 @@
     squares = jnp.where(diagonal, gram_a, 0.0)
     inv_row = 1.0 / jnp.sqrt(jnp.sum(squares, axis=0, keepdims=True) + EPSILON)
     inv_col = 1.0 / jnp.sqrt(jnp.sum(squares, axis=1, keepdims=True) + EPSILON)
-    solve_b = negative_inverse(c_gram * (gram_a * inv_row * inv_col))
-
-    mine = part_b[block(row, own_b), :]
-    for d in range(1, row_size):
-        partb_copy(d, d - 1).wait_recv()
+    solve_b = negative_inverse(c_gram * (gram_a * inv_row * inv_col), beside_b)
+
+    mine = sum_b[block(chip, own_b), :]
+    for d in range(1, chips):
+        partb_copy(d).wait_recv()
         mine = mine + recv_b[d - 1]
     b_out[...] = -exact_dot(mine * inv_row, solve_b)
 
+    half_copy.wait_send()
     pair_copy(0, row).wait_send()
     for d in range(1, chips):
+        partb_copy(d).wait_send()
         piece_copy(d, row).wait_send()
         pair_copy(d, chip_peer(chips - d)).wait_send()
     for d in range(1, row_size):
         gs_copy(d, d - 1).wait_send()
         gg_copy(d, row).wait_send()
-        partb_copy(d, d - 1).wait_send()
     for d in range(1, col_size):
         gramb_copy(d, col).wait_send()
         parta_copy(d, d - 1).wait_send()
@@ -416,8 +436,10 @@
             vmem((row_size - 1, own_g, rank), f32),
             vmem((rank, rank), f32),
             vmem((rank, cols), f32),
-            vmem((cols, rank), f32),
-            vmem((row_size - 1, own_b, rank), f32),
+            vmem((2, cols // 2, rank), f32),
+            vmem((cols // 2, rank), f32),
+            vmem((cols // 2, rank), f32),
+            vmem((row_size // 2, own_b, rank), f32),
             pltpu.SemaphoreType.DMA((depth,)),
             pltpu.SemaphoreType.DMA((2,)),
             chip_sem, chip_sem, chip_sem, chip_sem,
@@ -426,7 +448,8 @@
             col_sem, col_sem,
             row_sem, row_sem,
             row_sem, row_sem,
-            row_sem, row_sem,
+            pltpu.SemaphoreType.DMA((2,)),
+            chip_sem, chip_sem,
         ],
         compiler_params=pltpu.CompilerParams(
             collective_id=0, has_side_effects=True, vmem_limit_bytes=52 * 1024 * 1024

time: 41.6 us -> 45.4 us (1.091)
  Pallas kernels: 39.2 us -> 43.1 us
    pallas_call x1, Pallas kernels: 38.5 us -> 42.5 us  [per_device(): pl.pallas_call(functools.partial(kernel, row_size, col_size), out_shape=s...]
where the time goes in v6:
time: 45.4 us; the launch traced here: 45.2 us
  Pallas kernels  43.1 us (95%)
  local copies, waits for them, and re-layouts  1.45 us (3%)
  between operations  0.65 us (1%)
    pallas_call x1, Pallas kernels, per_device(): pl.pallas_call(functools.partial(kernel, row_size, col_size), out_shape=s...  42.5 us
    unnamed x4, local copies, waits for them, and re-layouts  1.45 us

profile of v6, /device:TPU:0, one launch (start us, length us, event | category | flops | bytes accessed | tf_op | source)
XLA Modules:
  0.0 45.2 jit_solution(14448788431606433673)
XLA Ops:
  0.6 0.0 copy-start
  0.6 0.7 %copy-done = f32[64,128]{1,0:T(8,128)S(1)} copy-done((f32[64,128]{1,0:T(8,128)S(1)}, f32[64,128]{1,0:T(8,128)}, u32[]{:S(2)}) %copy-start) | copy-done | bytes 32792
  1.4 0.0 copy-start.1
  1.4 0.7 %copy-done.1 = f32[12,128]{1,0:T(8,128)S(1)} copy-done((f32[12,128]{1,0:T(8,128)S(1)}, f32[12,128]{1,0:T(8,128)}, u32[]{:S(2)}) %copy-start.1) | copy-done | bytes 6168
  2.1 42.5 %shard_map.50 = (f32[128,128]{1,0:T(8,128)S(1)}, f32[64,128]{1,0:T(8,128)S(1)}) custom-call(f32[12,512,512]{2,1,0:T(8,128)} %tensor.1, f32[64,128]{1,0:T(8,128)S(1)} %copy-done, f32[12,128]{1,0:T(8,128)S(1)} %copy-done.1), custom_call_target="tpu_custom_call" | custom-call | flops 4831838208 | bytes 12582912 | tf_op jit(solution)/shard_map/pallas_call | solution.py:421
  44.6 0.7 %shard_map.51 = (f32[128,128]{1,0:T(8,128)}, f32[64,128]{1,0:T(8,128)}) custom-call(f32[128,128]{1,0:T(8,128)S(1)} %get-tuple-element.4.a_update, f32[64,128]{1,0:T(8,128)S(1)} %get-tuple-element.5.b_update), custom_call_target="tpu_custom_call" | custom-call | tf_op jit(solution)/shard_map/pallas_call | solution.py:464
Async XLA Ops:
  0.6 0.8 %copy-start = (f32[64,128]{1,0:T(8,128)S(1)}, f32[64,128]{1,0:T(8,128)}, u32[]{:S(2)}) copy-start(f32[64,128]{1,0:T(8,128)} %factor_b.1) | copy-start | bytes 98308
  1.4 0.7 %copy-start.1 = (f32[12,128]{1,0:T(8,128)S(1)}, f32[12,128]{1,0:T(8,128)}, u32[]{:S(2)}) copy-start(f32[12,128]{1,0:T(8,128)} %factor_c.1) | copy-start | bytes 18436

commit v7 on v5

--- a/solution.py
+++ b/solution.py
@@ -250,12 +250,6 @@
     for d in list(range(1, col_size)) + [0]:
         owner = col_peer(d)
         here = block(owner, own_a)
-        if d == 0:
-            for other in range(1, col_size):
-                gramb_copy(other, col_peer(col_size - other)).wait_recv()
-            gram_b = grams[0]
-            for index in range(1, col_size):
-                gram_b = gram_b + grams[index]
         total = jnp.zeros((own_a, rank), jnp.float32)
         for first in range(0, depth, group):
             span = slice(first, first + group)
@@ -269,6 +263,11 @@
         else:
             mine = total
 
+    for d in range(1, col_size):
+        gramb_copy(d, col_peer(col_size - d)).wait_recv()
+    gram_b = grams[0]
+    for index in range(1, col_size):
+        gram_b = gram_b + grams[index]
     solve_a = negative_inverse(c_gram * gram_b)
 
     for d in range(1, col_size):

time: 41.6 us -> 41 us (0.986)
  Pallas kernels: 39.2 us -> 38.6 us
    pallas_call x1, Pallas kernels: 38.5 us -> 37.9 us  [per_device(): pl.pallas_call(functools.partial(kernel, row_size, col_size), out_shape=s...]
where the time goes in v7:
time: 41 us; the launch traced here: 40.7 us
  Pallas kernels  38.6 us (94%)
  local copies, waits for them, and re-layouts  1.45 us (4%)
  between operations  0.65 us (2%)
    pallas_call x1, Pallas kernels, per_device(): pl.pallas_call(functools.partial(kernel, row_size, col_size), out_shape=s...  37.9 us
    unnamed x4, local copies, waits for them, and re-layouts  1.45 us

profile of v7, /device:TPU:0, one launch (start us, length us, event | category | flops | bytes accessed | tf_op | source)
XLA Modules:
  0.0 40.7 jit_solution(10935364185347324949)
XLA Ops:
  0.6 0.0 copy-start
  0.6 0.7 %copy-done = f32[64,128]{1,0:T(8,128)S(1)} copy-done((f32[64,128]{1,0:T(8,128)S(1)}, f32[64,128]{1,0:T(8,128)}, u32[]{:S(2)}) %copy-start) | copy-done | bytes 32792
  1.4 0.0 copy-start.1
  1.4 0.7 %copy-done.1 = f32[12,128]{1,0:T(8,128)S(1)} copy-done((f32[12,128]{1,0:T(8,128)S(1)}, f32[12,128]{1,0:T(8,128)}, u32[]{:S(2)}) %copy-start.1) | copy-done | bytes 6168
  2.1 37.9 %shard_map.50 = (f32[128,128]{1,0:T(8,128)S(1)}, f32[64,128]{1,0:T(8,128)S(1)}) custom-call(f32[12,512,512]{2,1,0:T(8,128)} %tensor.1, f32[64,128]{1,0:T(8,128)S(1)} %copy-done, f32[12,128]{1,0:T(8,128)S(1)} %copy-done.1), custom_call_target="tpu_custom_call" | custom-call | flops 4831838208 | bytes 12582912 | tf_op jit(solution)/shard_map/pallas_call | solution.py:400
  40.0 0.7 %shard_map.51 = (f32[128,128]{1,0:T(8,128)}, f32[64,128]{1,0:T(8,128)}) custom-call(f32[128,128]{1,0:T(8,128)S(1)} %get-tuple-element.4.a_update, f32[64,128]{1,0:T(8,128)S(1)} %get-tuple-element.5.b_update), custom_call_target="tpu_custom_call" | custom-call | tf_op jit(solution)/shard_map/pallas_call | solution.py:440
Async XLA Ops:
  0.6 0.8 %copy-start = (f32[64,128]{1,0:T(8,128)S(1)}, f32[64,128]{1,0:T(8,128)}, u32[]{:S(2)}) copy-start(f32[64,128]{1,0:T(8,128)} %factor_b.1) | copy-start | bytes 98308
  1.4 0.7 %copy-start.1 = (f32[12,128]{1,0:T(8,128)S(1)}, f32[12,128]{1,0:T(8,128)}, u32[]{:S(2)}) copy-start(f32[12,128]{1,0:T(8,128)} %factor_c.1) | copy-start | bytes 18436
